TPU v7x, 32 devices: a whole 2x2x4 slice. The times are simulated.
32 devices in a mesh: dp: 8 (over y, x, core), fsdp: 4 (over z).
Axes of the slice: x: 2, y: 2, z: 4, core: 2. Of those that a mesh axis runs over, the one named last changes fastest.
Arguments:
- images: bfloat16 [64, 197, 768], P(('dp', 'fsdp')), may hold values from -6 to 6
- gain_one: bfloat16 [768], P(('dp', 'fsdp')), may hold values from 0.5 to 1.5
- w_qkv: bfloat16 [768, 2304], P(('dp', 'fsdp')), may hold values from -0.21875 to 0.21875
- w_out: bfloat16 [768, 768], P(('dp', 'fsdp')), may hold values from -1.75 to 1.75
- gain_two: bfloat16 [768], P(('dp', 'fsdp')), may hold values from 0.5 to 1.5
- w_router: bfloat16 [768, 4], P(('dp', 'fsdp')), may hold values from -0.16992188 to 0.16992188
- w_in: bfloat16 [4, 768, 3072], P('fsdp', 'dp'), may hold values from -0.21875 to 0.21875
- w_back: bfloat16 [4, 3072, 768], P('fsdp', 'dp'), may hold values from -1.25 to 1.25
- choices: int32 [64, 197, 2], P(('dp', 'fsdp')), may hold values from 0 to 3, all different within a row
- priority: int32 [64, 197], P(('dp', 'fsdp')), may hold values from 0 to 196, each once within a row
- cotangent: bfloat16 [64, 197, 768], P(('dp', 'fsdp')), may hold values from -6 to 6
Outputs:
- output: bfloat16 [64, 197, 768], P(('dp', 'fsdp'))
- input_grad: float32 [64, 197, 768], P(('dp', 'fsdp'))
- grad_gain_one: float32 [768], P(('dp', 'fsdp'))
- grad_qkv: float32 [768, 2304], P(('dp', 'fsdp'))
- grad_out: float32 [768, 768], P(('dp', 'fsdp'))
- grad_gain_two: float32 [768], P(('dp', 'fsdp'))
- grad_router: float32 [768, 4], P(('dp', 'fsdp'))
- grad_in: float32 [4, 768, 3072], P('fsdp', 'dp')
- grad_back: float32 [4, 3072, 768], P('fsdp', 'dp')
Inputs may be any that keep to these rules, and one draw needn't show every extreme that they name: `choices`: the two experts of a token differ. `priority`: each row orders the 197 tokens of one routing group, each number once.
All inputs are finite; a program needn't handle non-finite values.
Results may differ from a plain program's by a relative error of at most 0.018.
Values may be sent and summed in bfloat16 or wider, within the bound.
A program may use at most 192 MiB of HBM per device.

v0:
```python
from functools import partial

import jax
import jax.numpy as jnp
from jax import lax
from jax.sharding import PartitionSpec as P

D = 768
HEADS = 12
HEAD_DIM = 64
FF = 3072
SEQ = 197
IMG_MB = 1
MICRO = 2
EXP_DEV = 1


highest = lax.Precision.HIGHEST
epsilon = 1e-06


def norm_parts(token_rows):
    centred = token_rows - jnp.mean(token_rows, axis=-1, keepdims=True)
    inverse = lax.rsqrt(jnp.mean(centred * centred, axis=-1, keepdims=True) + epsilon)
    return (centred * inverse, inverse)


def norm_back(grad_normed, normed, inverse):
    first_term = jnp.mean(grad_normed, axis=-1, keepdims=True)
    second_term = normed * jnp.mean(grad_normed * normed, axis=-1, keepdims=True)
    return inverse * (grad_normed - first_term - second_term)


def route_slots(chosen, ranking, expert_count, capacity):
    earlier_mask = ranking[None, :] < ranking[:, None]
    first_same = chosen[None, :, 0] == chosen[:, None, 0]
    second_same = chosen[None, :, 1] == chosen[:, None, 1]
    first_rank = jnp.sum((earlier_mask & first_same).astype(jnp.int32), axis=1)
    second_rank = jnp.sum((earlier_mask & second_same).astype(jnp.int32), axis=1)
    first_load = jnp.sum((chosen[None, :, 0] == chosen[:, None, 1]).astype(jnp.int32), axis=1)
    position = jnp.stack([first_rank, second_rank + first_load], axis=1)
    kept_mask = position < capacity
    slot_index = jnp.where(kept_mask, chosen * capacity + position, expert_count * capacity)
    return slot_index


def fetch_weights(gain_one, w_qkv, w_out, gain_two, w_router, w_in, w_back):
    layer_set = (
        lax.all_gather(gain_one, ("dp", "fsdp"), axis=0, tiled=True),
        lax.all_gather(w_qkv, ("dp", "fsdp"), axis=0, tiled=True),
        lax.all_gather(w_out, ("dp", "fsdp"), axis=0, tiled=True),
        lax.all_gather(gain_two, ("dp", "fsdp"), axis=0, tiled=True),
        lax.all_gather(w_router, ("dp", "fsdp"), axis=0, tiled=True),
    )
    expert_set = (
        lax.all_gather(w_in, "dp", axis=1, tiled=True),
        lax.all_gather(w_back, "dp", axis=1, tiled=True),
    )
    return (layer_set, expert_set)


def per_device(
    images, gain_one, w_qkv, w_out, gain_two, w_router, w_in, w_back, choices, priority, cotangent
):
    expert_count = w_router.shape[1]
    token_count = IMG_MB * SEQ
    capacity = (42 * token_count + 20 * expert_count - 1) // (20 * expert_count)
    score_scale = HEAD_DIM ** (-0.5)
    total_gain_one = jnp.zeros((D,), jnp.float32)
    total_qkv = jnp.zeros((D, 3 * D), jnp.float32)
    total_out = jnp.zeros((D, D), jnp.float32)
    total_gain_two = jnp.zeros((D,), jnp.float32)
    total_router = jnp.zeros((D, expert_count), jnp.float32)
    total_in = jnp.zeros((EXP_DEV, D, FF), jnp.float32)
    total_back = jnp.zeros((EXP_DEV, FF, D), jnp.float32)
    out_blocks = []
    grad_blocks = []
    for micro_step in range(MICRO):
        first_image = micro_step * IMG_MB
        forward_weights = fetch_weights(gain_one, w_qkv, w_out, gain_two, w_router, w_in, w_back)
        layer_set, expert_set = forward_weights
        full_gain_one, full_qkv, full_out, full_gain_two, full_router = layer_set
        full_in, full_back = expert_set
        token_rows = (
            images[first_image : first_image + IMG_MB].reshape(token_count, D).astype(jnp.float32)
        )
        chosen = choices[first_image : first_image + IMG_MB].reshape(token_count, 2)
        ranking = priority[micro_step]
        gain_one_wide = full_gain_one.astype(jnp.float32)
        gain_two_wide = full_gain_two.astype(jnp.float32)
        normed_one, inverse_one = norm_parts(token_rows)
        first_in = (normed_one * gain_one_wide).astype(jnp.bfloat16)
        mixed_rows = jnp.dot(first_in, full_qkv, preferred_element_type=jnp.float32).astype(
            jnp.bfloat16
        )
        mixed_rows = mixed_rows.reshape(IMG_MB, SEQ, 3, HEADS, HEAD_DIM)
        queries = mixed_rows[:, :, 0]
        key_rows = mixed_rows[:, :, 1]
        value_rows = mixed_rows[:, :, 2]
        scores = (
            jnp.einsum("bqhd,bkhd->bhqk", queries, key_rows, preferred_element_type=jnp.float32)
            * score_scale
        )
        top_score = jnp.max(scores, axis=-1, keepdims=True)
        log_total = top_score + jnp.log(
            jnp.sum(jnp.exp(scores - top_score), axis=-1, keepdims=True)
        )
        probs_low = jnp.exp(scores - log_total).astype(jnp.bfloat16)
        attended = jnp.einsum(
            "bhqk,bkhd->bqhd", probs_low, value_rows, preferred_element_type=jnp.float32
        )
        attended = attended.astype(jnp.bfloat16).reshape(token_count, D)
        residual = token_rows + jnp.dot(attended, full_out, preferred_element_type=jnp.float32)
        normed_two, inverse_two = norm_parts(residual)
        second_in = (normed_two * gain_two_wide).astype(jnp.bfloat16)
        logits = jnp.dot(second_in, full_router, preferred_element_type=jnp.float32)
        router_probs = jax.nn.softmax(logits, axis=-1)
        expert_ids = lax.broadcasted_iota(jnp.int32, (token_count, 2, expert_count), 2)
        pick_mask = (chosen[:, :, None] == expert_ids).astype(jnp.float32)
        gate_values = jnp.sum(pick_mask * router_probs[:, None, :], axis=2)
        slot_index = route_slots(chosen, ranking, expert_count, capacity)
        buffer = jnp.zeros((expert_count * capacity + 1, D), jnp.bfloat16)
        buffer = buffer.at[slot_index.reshape(-1)].set(jnp.repeat(second_in, 2, axis=0))
        buffer = buffer[:-1].reshape(expert_count, capacity, D)
        received = lax.all_to_all(buffer, "fsdp", split_axis=0, concat_axis=0, tiled=True)
        item_count = received.shape[1]
        grouped = received.reshape(-1, EXP_DEV, item_count, D)
        hidden = jnp.einsum("secd,edf->secf", grouped, full_in, preferred_element_type=jnp.float32)
        activated = jax.nn.gelu(hidden, approximate=True).astype(jnp.bfloat16)
        produced = jnp.einsum(
            "secf,efd->secd", activated, full_back, preferred_element_type=jnp.float32
        )
        produced = produced.astype(jnp.bfloat16).reshape(-1, item_count, D)
        returned = lax.all_to_all(produced, "fsdp", split_axis=0, concat_axis=0, tiled=True)
        returned, received, hidden, activated = (
            returned,
            received,
            hidden.reshape(-1, item_count, FF),
            activated.reshape(-1, item_count, FF),
        )
        padded = jnp.concatenate([returned.reshape(-1, D), jnp.zeros((1, D), jnp.bfloat16)], axis=0)
        picked = padded[slot_index].astype(jnp.float32)
        combined = jnp.sum(picked * gate_values[:, :, None], axis=1)
        out_blocks.append((residual + combined).astype(jnp.bfloat16).reshape(IMG_MB, SEQ, D))
        backward_weights = fetch_weights(gain_one, w_qkv, w_out, gain_two, w_router, w_in, w_back)
        layer_set, expert_set = backward_weights
        full_gain_one, full_qkv, full_out, full_gain_two, full_router = layer_set
        full_in, full_back = expert_set
        upstream = (
            cotangent[first_image : first_image + IMG_MB]
            .reshape(token_count, D)
            .astype(jnp.float32)
        )
        grad_gates = jnp.sum(upstream[:, None, :] * picked, axis=2)
        slot_grads = (
            (gate_values[:, :, None] * upstream[:, None, :]).astype(jnp.bfloat16).reshape(-1, D)
        )
        grad_buffer = jnp.zeros((expert_count * capacity + 1, D), jnp.bfloat16)
        grad_buffer = grad_buffer.at[slot_index.reshape(-1)].set(slot_grads)
        grad_buffer = grad_buffer[:-1].reshape(expert_count, capacity, D)
        arrived = lax.all_to_all(grad_buffer, "fsdp", split_axis=0, concat_axis=0, tiled=True)
        item_count = arrived.shape[1]
        arrived_grouped = arrived.reshape(-1, EXP_DEV, item_count, D)
        grad_active = jnp.einsum(
            "secd,efd->secf", arrived_grouped, full_back, preferred_element_type=jnp.float32
        )
        hidden_grouped = hidden.reshape(-1, EXP_DEV, item_count, FF)
        gelu_pull = jax.vjp(partial(jax.nn.gelu, approximate=True), hidden_grouped)[1]
        grad_hidden = gelu_pull(grad_active)[0].astype(jnp.bfloat16)
        active_grouped = activated.reshape(-1, EXP_DEV, item_count, FF)
        total_back = total_back + jnp.einsum(
            "secf,secd->efd", active_grouped, arrived_grouped, preferred_element_type=jnp.float32
        )
        input_grouped = received.reshape(-1, EXP_DEV, item_count, D)
        total_in = total_in + jnp.einsum(
            "secd,secf->edf", input_grouped, grad_hidden, preferred_element_type=jnp.float32
        )
        grad_sent = jnp.einsum(
            "secf,edf->secd", grad_hidden, full_in, preferred_element_type=jnp.float32
        )
        grad_sent = grad_sent.astype(jnp.bfloat16).reshape(-1, item_count, D)
        grad_slots = lax.all_to_all(grad_sent, "fsdp", split_axis=0, concat_axis=0, tiled=True)
        grad_padded = jnp.concatenate(
            [grad_slots.reshape(-1, D), jnp.zeros((1, D), jnp.bfloat16)], axis=0
        )
        grad_second = jnp.sum(grad_padded[slot_index].astype(jnp.float32), axis=1)
        grad_probs = jnp.sum(pick_mask * grad_gates[:, :, None], axis=1)
        grad_logits = router_probs * (
            grad_probs - jnp.sum(router_probs * grad_probs, axis=1, keepdims=True)
        )
        total_router = total_router + jnp.dot(
            second_in.astype(jnp.float32).T, grad_logits, precision=highest
        )
        grad_second = grad_second + jnp.dot(
            grad_logits, full_router.astype(jnp.float32).T, precision=highest
        )
        total_gain_two = total_gain_two + jnp.sum(grad_second * normed_two, axis=0)
        grad_residual = upstream + norm_back(grad_second * gain_two_wide, normed_two, inverse_two)
        branch_grad = grad_residual.astype(jnp.bfloat16)
        total_out = total_out + jnp.dot(attended.T, branch_grad, preferred_element_type=jnp.float32)
        grad_attended = jnp.dot(branch_grad, full_out.T, preferred_element_type=jnp.float32)
        grad_attended = grad_attended.astype(jnp.bfloat16).reshape(IMG_MB, SEQ, HEADS, HEAD_DIM)
        scores_again = (
            jnp.einsum("bqhd,bkhd->bhqk", queries, key_rows, preferred_element_type=jnp.float32)
            * score_scale
        )
        probs_exact = jnp.exp(scores_again - log_total)
        grad_values = jnp.einsum(
            "bhqk,bqhd->bkhd",
            probs_exact.astype(jnp.bfloat16),
            grad_attended,
            preferred_element_type=jnp.float32,
        ).astype(jnp.bfloat16)
        grad_weighting = jnp.einsum(
            "bqhd,bkhd->bhqk", grad_attended, value_rows, preferred_element_type=jnp.float32
        )
        grad_scores = probs_exact * (
            grad_weighting - jnp.sum(probs_exact * grad_weighting, axis=-1, keepdims=True)
        )
        grad_scores = grad_scores.astype(jnp.bfloat16)
        grad_queries = (
            jnp.einsum("bhqk,bkhd->bqhd", grad_scores, key_rows, preferred_element_type=jnp.float32)
            * score_scale
        ).astype(jnp.bfloat16)
        grad_keys = (
            jnp.einsum("bhqk,bqhd->bkhd", grad_scores, queries, preferred_element_type=jnp.float32)
            * score_scale
        ).astype(jnp.bfloat16)
        grad_mixed = jnp.stack([grad_queries, grad_keys, grad_values], axis=2).reshape(
            token_count, 3 * D
        )
        total_qkv = total_qkv + jnp.dot(first_in.T, grad_mixed, preferred_element_type=jnp.float32)
        grad_first = jnp.dot(grad_mixed, full_qkv.T, preferred_element_type=jnp.float32)
        total_gain_one = total_gain_one + jnp.sum(grad_first * normed_one, axis=0)
        grad_tokens = grad_residual + norm_back(grad_first * gain_one_wide, normed_one, inverse_one)
        grad_blocks.append(grad_tokens.reshape(IMG_MB, SEQ, D))
    layer_grads = (
        lax.psum_scatter(total_gain_one, ("dp", "fsdp"), scatter_dimension=0, tiled=True),
        lax.psum_scatter(total_qkv, ("dp", "fsdp"), scatter_dimension=0, tiled=True),
        lax.psum_scatter(total_out, ("dp", "fsdp"), scatter_dimension=0, tiled=True),
        lax.psum_scatter(total_gain_two, ("dp", "fsdp"), scatter_dimension=0, tiled=True),
        lax.psum_scatter(total_router, ("dp", "fsdp"), scatter_dimension=0, tiled=True),
    )
    expert_grads = (
        lax.psum_scatter(
            total_in.astype(jnp.bfloat16), "dp", scatter_dimension=1, tiled=True
        ).astype(jnp.float32),
        lax.psum_scatter(
            total_back.astype(jnp.bfloat16), "dp", scatter_dimension=1, tiled=True
        ).astype(jnp.float32),
    )
    return (
        jnp.concatenate(out_blocks, axis=0),
        jnp.concatenate(grad_blocks, axis=0),
        layer_grads[0],
        layer_grads[1],
        layer_grads[2],
        layer_grads[3],
        layer_grads[4],
        expert_grads[0],
        expert_grads[1],
    )


def solution(mesh):
    placed = (
        P(("dp", "fsdp"), None, None),
        P(("dp", "fsdp")),
        P(("dp", "fsdp"), None),
        P(("dp", "fsdp"), None),
        P(("dp", "fsdp")),
        P(("dp", "fsdp"), None),
        P("fsdp", "dp", None),
        P("fsdp", "dp", None),
        P(("dp", "fsdp"), None, None),
        P(("dp", "fsdp"), None),
        P(("dp", "fsdp"), None, None),
    )
    return jax.shard_map(
        per_device,
        mesh=mesh,
        in_specs=placed,
        out_specs=(
            P(("dp", "fsdp"), None, None),
            P(("dp", "fsdp"), None, None),
            P(("dp", "fsdp")),
            P(("dp", "fsdp"), None),
            P(("dp", "fsdp"), None),
            P(("dp", "fsdp")),
            P(("dp", "fsdp"), None),
            P("fsdp", "dp", None),
            P("fsdp", "dp", None),
        ),
        check_vma=False,
    )
```

profile of v0, /device:TPU:0, one launch (start us, length us, event | category | flops | bytes accessed | tf_op | source)
XLA Modules:
  0.0 702.9 jit_solution(15108654345816898157)
XLA Ops:
  13.7 42.2 %all-reduce.10 = (bf16[768]{0:T(1024)(128)(2,1)S(1)}, bf16[768]{0:T(1024)(128)(2,1)S(1)}) all-reduce(bf16[768]{0:T(1024)(128)(2,1)S(1)} %dynamic-update-slice, bf16[768]{0:T(1024)(128)(2,1)S(1)} %dynamic-update-slice.1), channel_id=1, replica_groups=mesh['dp'=8,'fsdp'=4] {'dp','fsdp'}, use_global_device_ids=true, to_apply=%add.4 | all-reduce | flops 1536 | bytes 6144
  63.5 66.6 %all-gather = bf16[32,24,4]{1,2,0:T(4,128)(2,1)S(1)} all-gather(bf16[1,24,4]{1,2,0:T(4,128)(2,1)S(1)} %bitcast.487), channel_id=1, replica_groups=mesh['dp'=8,'fsdp'=4] {'dp','fsdp'}, dimensions={0}, use_global_device_ids=true | all-gather | bytes 6336 | tf_op jit(solution)/shard_map/all_gather | solution.py:53
  178.9 7.2 %fusion.38 = f32[4,104,3072]{2,1,0:T(8,128)} fusion(bf16[4,104,768]{2,1,0:T(8,128)(2,1)} %all-to-all-done, bf16[1,768,3072]{2,1,0:T(8,128)(2,1)} %all-gather.10.cloned.1.call-done), kind=kOutput, calls=%fused_computation.59 | convolution fusion | flops 1962934272 | bytes 10469376 | tf_op jit(solution)/shard_map/secd,edf->secf/dot_general | solution.py:128
  186.1 4.8 all-to-all-done.4
  190.9 19.3 %all-gather.12.cloned.1.call-done = bf16[1,3072,768]{2,1,0:T(8,128)(2,1)} async-done(((bf16[1,384,768]{2,1,0:T(8,128)(2,1)}), bf16[1,3072,768]{2,1,0:T(8,128)(2,1)}) %all-gather.12.cloned.1.call-update) | async-done | bytes 4718608 | tf_op jit(solution)/shard_map/all_gather | solution.py:57
  210.2 8.1 %fusion.44 = bf16[4,104,3072]{2,1,0:T(8,128)(2,1)S(1)} fusion(f32[4,104,3072]{2,1,0:T(8,128)} %fusion.38, bf16[4,104,768]{2,1,0:T(8,128)(2,1)S(1)} %all-to-all-done.4, bf16[1,3072,768]{2,1,0:T(8,128)(2,1)} %all-gather.12.cloned.1.call-done), kind=kOutput, calls=%fused_computation.65 | convolution fusion | flops 1988493312 | bytes 13025280 | tf_op jit(solution)/shard_map/secd,efd->secf/dot_general | solution.py:164
  222.9 4.6 all-to-all-start.5
  227.5 7.9 %fusion.65 = bf16[4,104,768]{2,1,0:T(8,128)(2,1)} fusion(bf16[1,3072,768]{2,1,0:T(8,128)(2,1)} %all-gather.12.cloned.1.call-done, f32[4,104,3072]{2,1,0:T(8,128)} %fusion.38), kind=kOutput, calls=%fused_computation.87 | convolution fusion | flops 1974755328 | bytes 10469376 | tf_op jit(solution)/shard_map/secf,efd->secd/dot_general | solution.py:130
  235.4 9.5 %all-to-all-done.5 = bf16[4,104,768]{2,1,0:T(8,128)(2,1)S(1)} async-done(((bf16[4,104,768]{2,1,0:T(8,128)(2,1)}), bf16[4,104,768]{2,1,0:T(8,128)(2,1)S(1)}, u32[]{:S(2)}, u32[]{:S(2)}) %all-to-all-start.5) | async-done | bytes 639008 | tf_op jit(solution)/shard_map/all_to_all | solution.py:182
  258.7 7.9 %all-to-all-done.1 = bf16[4,104,768]{2,1,0:T(8,128)(2,1)} async-done(((bf16[4,104,768]{2,1,0:T(8,128)(2,1)}), bf16[4,104,768]{2,1,0:T(8,128)(2,1)}, u32[]{:S(2)}, u32[]{:S(2)}) %all-to-all-start.1) | async-done | bytes 639008 | tf_op jit(solution)/shard_map/all_to_all | solution.py:134
  273.3 4.7 multiply_reduce_fusion.5
  314.0 5.3 all-to-all-done.2
  322.8 8.1 %fusion.206 = f32[768,3072,1]{1,0,2:T(8,128)} fusion(bf16[4,104,768]{2,1,0:T(8,128)(2,1)} %all-to-all-done, bf16[4,104,3072]{2,1,0:T(8,128)(2,1)} %copy-done.111), kind=kOutput, calls=%fused_computation.326 | convolution fusion | flops 1962934272 | bytes 12632064 | tf_op jit(solution)/shard_map/secd,secf->edf/dot_general | solution.py:175
  330.9 7.0 %fusion.36 = f32[4,104,3072]{2,1,0:T(8,128)} fusion(bf16[4,104,768]{2,1,0:T(8,128)(2,1)} %all-to-all-done.2, bf16[1,768,3072]{2,1,0:T(8,128)(2,1)} %all-gather.10.cloned.1.call-done), kind=kOutput, calls=%fused_computation.57 | convolution fusion | flops 1962934272 | bytes 10469376 | tf_op jit(solution)/shard_map/secd,edf->secf/dot_general | solution.py:128
  339.2 8.3 %fusion.49 = bf16[4,104,3072]{2,1,0:T(8,128)(2,1)S(1)} fusion(f32[4,104,3072]{2,1,0:T(8,128)} %fusion.36, bf16[4,104,768]{2,1,0:T(8,128)(2,1)S(1)} %all-to-all-done.6, bf16[1,3072,768]{2,1,0:T(8,128)(2,1)} %all-gather.12.cloned.1.call-done), kind=kOutput, calls=%fused_computation.66 | convolution fusion | flops 1988493312 | bytes 13025280 | tf_op jit(solution)/shard_map/secd,efd->secf/dot_general | solution.py:164
  348.9 5.6 fusion.40
  355.6 5.0 fusion.54
  360.6 8.6 %fusion.41 = bf16[1,3072,768]{2,1,0:T(8,128)(2,1)} fusion(bf16[4,104,768]{2,1,0:T(8,128)(2,1)S(1)} %copy-done.52, f32[3072,768,1]{1,0,2:T(8,128)S(1)} %fusion.54, f32[4,104,3072]{2,1,0:T(8,128)} %fusion.36), kind=kOutput, calls=%fused_computation.62 | convolution fusion | flops 1979154432 | bytes 19906560 | tf_op jit(solution)/shard_map/secf,secd->efd/dot_general | solution.py:171
  376.2 6.6 fusion.62
  391.0 8.0 %fusion.70 = bf16[4,104,768]{2,1,0:T(8,128)(2,1)} fusion(bf16[1,3072,768]{2,1,0:T(8,128)(2,1)} %all-gather.12.cloned.1.call-done, f32[4,104,3072]{2,1,0:T(8,128)} %fusion.36), kind=kOutput, calls=%fused_computation.88 | convolution fusion | flops 1974755328 | bytes 10469376 | tf_op jit(solution)/shard_map/secf,efd->secd/dot_general | solution.py:130
  433.9 5.0 multiply_reduce_fusion.4
  479.4 40.0 %all-reduce.9 = (f32[768]{0:T(1024)S(1)}, f32[768]{0:T(1024)S(1)}, f32[768,4]{0,1:T(4,128)S(1)}) all-reduce(f32[768]{0:T(1024)S(1)} %add.301, f32[768]{0:T(1024)S(1)} %add.304, f32[768,4]{0,1:T(4,128)S(1)} %convolution_add_fusion.6), channel_id=2, replica_groups=mesh['dp'=8,'fsdp'=4] {'dp','fsdp'}, use_global_device_ids=true, to_apply=%region_50.51.clone | all-reduce | flops 4608 | bytes 36864
  525.6 44.7 %reduce-scatter.8.cloned.1.call-done = f32[24,768]{1,0:T(8,128)} async-done(((f32[768,768]{1,0:T(8,128)}), f32[24,768]{1,0:T(8,128)}) %reduce-scatter.8.cloned.1.call-update) | async-done | bytes 73744 | tf_op jit(solution)/shard_map/reduce_scatter | solution.py:240
  570.3 125.3 %reduce-scatter.6.cloned.1.call-done = f32[24,2304]{1,0:T(8,128)} async-done(((f32[768,2304]{1,0:T(8,128)}), f32[24,2304]{1,0:T(8,128)}) %reduce-scatter.6.cloned.1.call-update) | async-done | bytes 221200 | tf_op jit(solution)/shard_map/reduce_scatter | solution.py:239
  (426 shorter events, 226.5 us)
Async XLA Ops:
  7.2 50.5 %copy-start.45 = (bf16[2,197,768]{2,0,1:T(2,128)(2,1)S(1)}, bf16[2,197,768]{2,0,1:T(2,128)(2,1)}, u32[]{:S(2)}) copy-start(bf16[2,197,768]{2,0,1:T(2,128)(2,1)} %param.21) | copy-start | bytes 1815556
  7.2 127.9 %all-gather.6.cloned.1.call-start = ((), (), s32[]{:S(2)}) async-start(), calls=%async_computation.12 | async-start | bytes 3649536 | tf_op jit(solution)/shard_map/all_gather | solution.py:50
  7.9 134.0 %all-gather.8.cloned.1.call-start = ((), (), s32[]{:S(2)}) async-start(), calls=%async_computation.13 | async-start | bytes 1216512 | tf_op jit(solution)/shard_map/all_gather | solution.py:51
  8.7 170.2 %all-gather.10.cloned.1.call-start = ((), (), s32[]{:S(2)}) async-start(), calls=%async_computation.14 | async-start | bytes 5308416 | tf_op jit(solution)/shard_map/all_gather | solution.py:56
  9.4 200.7 %all-gather.12.cloned.1.call-start = ((), (), s32[]{:S(2)}) async-start(), calls=%async_computation.15 | async-start | bytes 5308416 | tf_op jit(solution)/shard_map/all_gather | solution.py:57
  55.9 88.2 %copy-start.55 = (f32[768]{0:T(1024)}, f32[768]{0:T(1024)S(1)}, u32[]{:S(2)}) copy-start(f32[768]{0:T(1024)S(1)} %convert_element_type.288) | copy-start | bytes 9220
  60.3 69.8 %copy-start.99 = (s32[2,197,2]{1,2,0:T(2,128)S(1)}, s32[2,197,2]{1,2,0:T(2,128)}, u32[]{:S(2)}) copy-start(s32[2,197,2]{1,2,0:T(2,128)} %param.19) | copy-start | bytes 9460
  60.3 70.7 %copy-start.46 = (bf16[2,197,768]{2,0,1:T(2,128)(2,1)S(1)}, bf16[2,197,768]{2,0,1:T(2,128)(2,1)}, u32[]{:S(2)}) copy-start(bf16[2,197,768]{2,0,1:T(2,128)(2,1)} %param.11) | copy-start | bytes 1815556
  155.7 17.3 %all-to-all-start = ((bf16[4,104,768]{2,1,0:T(8,128)(2,1)}), bf16[4,104,768]{2,1,0:T(8,128)(2,1)}, u32[]{:S(2)}, u32[]{:S(2)}) async-start(bf16[4,104,768]{2,1,0:T(8,128)(2,1)} %bitcast.467), calls=%async_computation | async-start | bytes 1277952 | tf_op jit(solution)/shard_map/all_to_all | solution.py:125
  166.5 116.2 %copy-start.57 = (f32[197,4]{0,1:T(4,128)}, f32[197,4]{0,1:T(4,128)S(1)}, u32[]{:S(2)}) copy-start(f32[197,4]{0,1:T(4,128)S(1)} %fusion.171) | copy-start | bytes 9460
  173.0 17.9 %all-to-all-start.4 = ((bf16[4,104,768]{2,1,0:T(8,128)(2,1)}), bf16[4,104,768]{2,1,0:T(8,128)(2,1)S(1)}, u32[]{:S(2)}, u32[]{:S(2)}) async-start(bf16[4,104,768]{2,1,0:T(8,128)(2,1)} %bitcast.61), calls=%async_computation.4 | async-start | bytes 1277952 | tf_op jit(solution)/shard_map/all_to_all | solution.py:161
  190.9 27.4 %copy-start.49 = (bf16[4,104,768]{2,1,0:T(8,128)(2,1)}, bf16[4,104,768]{2,1,0:T(8,128)(2,1)S(1)}, u32[]{:S(2)}) copy-start(bf16[4,104,768]{2,1,0:T(8,128)(2,1)S(1)} %all-to-all-done.4) | copy-start | bytes 1916932
  222.9 22.0 %all-to-all-start.5 = ((bf16[4,104,768]{2,1,0:T(8,128)(2,1)}), bf16[4,104,768]{2,1,0:T(8,128)(2,1)S(1)}, u32[]{:S(2)}, u32[]{:S(2)}) async-start(bf16[4,104,768]{2,1,0:T(8,128)(2,1)} %fusion.59), calls=%async_computation.5 | async-start | bytes 1277952 | tf_op jit(solution)/shard_map/all_to_all | solution.py:182
  235.4 16.5 %copy-start.12 = (bf16[1,197,768]{2,1,0:T(8,128)(2,1)S(1)}, bf16[1,197,768]{2,1,0:T(8,128)(2,1)}, u32[]{:S(2)}) copy-start(bf16[1,197,768]{2,1,0:T(8,128)(2,1)} %copy-done.11) | copy-start | bytes 907780
  245.7 21.0 %all-to-all-start.1 = ((bf16[4,104,768]{2,1,0:T(8,128)(2,1)}), bf16[4,104,768]{2,1,0:T(8,128)(2,1)}, u32[]{:S(2)}, u32[]{:S(2)}) async-start(bf16[4,104,768]{2,1,0:T(8,128)(2,1)} %fusion.65), calls=%async_computation.1 | async-start | bytes 1277952 | tf_op jit(solution)/shard_map/all_to_all | solution.py:134
  298.2 21.1 %all-to-all-start.2 = ((bf16[4,104,768]{2,1,0:T(8,128)(2,1)}), bf16[4,104,768]{2,1,0:T(8,128)(2,1)}, u32[]{:S(2)}, u32[]{:S(2)}) async-start(bf16[4,104,768]{2,1,0:T(8,128)(2,1)} %bitcast.466), calls=%async_computation.2 | async-start | bytes 1277952 | tf_op jit(solution)/shard_map/all_to_all | solution.py:125
  309.1 21.9 %copy-start.59 = (f32[197,4]{0,1:T(4,128)}, f32[197,4]{0,1:T(4,128)S(1)}, u32[]{:S(2)}) copy-start(f32[197,4]{0,1:T(4,128)S(1)} %fusion.173) | copy-start | bytes 9460
  319.3 19.9 %all-to-all-start.6 = ((bf16[4,104,768]{2,1,0:T(8,128)(2,1)}), bf16[4,104,768]{2,1,0:T(8,128)(2,1)S(1)}, u32[]{:S(2)}, u32[]{:S(2)}) async-start(bf16[4,104,768]{2,1,0:T(8,128)(2,1)} %bitcast.468), calls=%async_computation.6 | async-start | bytes 1277952 | tf_op jit(solution)/shard_map/all_to_all | solution.py:161
  322.8 198.5 %reduce-scatter.10.cloned.1.call-start = ((), (), s32[]{:S(2)}) async-start(), calls=%async_computation.18 | async-start | bytes 5308416 | tf_op jit(solution)/shard_map/reduce_scatter | solution.py:245
  354.5 168.9 %reduce-scatter.12.cloned.1.call-start = ((), (), s32[]{:S(2)}) async-start(), calls=%async_computation.19 | async-start | bytes 5308416 | tf_op jit(solution)/shard_map/reduce_scatter | solution.py:248
  382.7 20.7 %all-to-all-start.7 = ((bf16[4,104,768]{2,1,0:T(8,128)(2,1)}), bf16[4,104,768]{2,1,0:T(8,128)(2,1)}, u32[]{:S(2)}, u32[]{:S(2)}) async-start(bf16[4,104,768]{2,1,0:T(8,128)(2,1)} %fusion.62), calls=%async_computation.7 | async-start | bytes 1277952 | tf_op jit(solution)/shard_map/all_to_all | solution.py:182
  403.5 23.7 %all-to-all-start.3 = ((bf16[4,104,768]{2,1,0:T(8,128)(2,1)}), bf16[4,104,768]{2,1,0:T(8,128)(2,1)}, u32[]{:S(2)}, u32[]{:S(2)}) async-start(bf16[4,104,768]{2,1,0:T(8,128)(2,1)} %fusion.70), calls=%async_computation.3 | async-start | bytes 1277952 | tf_op jit(solution)/shard_map/all_to_all | solution.py:134
  407.6 162.7 %reduce-scatter.8.cloned.1.call-start = ((), (), s32[]{:S(2)}) async-start(), calls=%async_computation.17 | async-start | bytes 2433024 | tf_op jit(solution)/shard_map/reduce_scatter | solution.py:240
  447.5 248.1 %reduce-scatter.6.cloned.1.call-start = ((), (), s32[]{:S(2)}) async-start(), calls=%async_computation.16 | async-start | bytes 7299072 | tf_op jit(solution)/shard_map/reduce_scatter | solution.py:239
  (107 other events, 472.1 us)
Sparse Core Ops, SparseCore 0:
  10.8 63.1 all-gather.5
  76.8 52.8 all-gather.7
  131.6 37.8 all-gather.9
  171.2 38.9 all-gather.11
  354.7 53.1 reduce-scatter.9
  411.5 53.8 reduce-scatter.11
  471.3 98.9 reduce-scatter.7
  577.5 118.0 reduce-scatter.5
where the time goes:
time: 709 us; the launch traced here: 703 us
  waiting for transfers between devices  227 us (32%)
  blocking collectives  149 us (21%)
  matrix products  137 us (19%)
  local copies, waits for them, and re-layouts  92.2 us (13%)
  other arithmetic  46.8 us (7%)
  starting transfers between devices  34.1 us (5%)
  between operations  16.1 us (2%)
    reduce_scatter x1, waiting for transfers between devices, per_device(): lax.psum_scatter(total_qkv, ('dp', 'fsdp'), scatter_dimension=0, tiled=True)  125 us
    unnamed x2, blocking collectives  82.2 us
    all_gather x1, blocking collectives, fetch_weights(): lax.all_gather(w_router, ('dp', 'fsdp'), axis=0, tiled=True)  66.6 us
    reduce_scatter x1, waiting for transfers between devices, per_device(): lax.psum_scatter(total_out, ('dp', 'fsdp'), scatter_dimension=0, tiled=True)  44.7 us
    unnamed x240, local copies, waits for them, and re-layouts  24.8 us
    all_gather x1, waiting for transfers between devices, fetch_weights(): lax.all_gather(w_back, 'dp', axis=1, tiled=True)  19.3 us
    dot_general x2, matrix products, per_device(): jnp.einsum('secd,efd->secf', arrived_grouped, full_back, preferred_elemen...  16.4 us
    dot_general x2, matrix products, per_device(): jnp.einsum('secf,efd->secd', activated, full_back, preferred_element_type...  15.8 us
  transfers between devices with their start and end apart: 16, of which 10 were waited for; matrix products, arithmetic and copies ran while one was open for 29% of the time, Pallas kernels for 0%

commit v1 on v0

v1 whole, which is shorter than its diff:
```python
import math
from functools import partial

import jax
import jax.numpy as jnp
from jax import lax
from jax.experimental import pallas as pl
from jax.experimental.pallas import tpu as pltpu
from jax.sharding import PartitionSpec as P

f32, bf16 = jnp.float32, jnp.bfloat16

MESH = pl.DeviceIdType.MESH
ANY = pl.BlockSpec(memory_space=pl.ANY)
VM = pl.BlockSpec(memory_space=pltpu.VMEM)


class Place:
    def __init__(self, ndp, nz):
        self.ndp, self.nz, self.chips = ndp, nz, ndp // 2
        self.dp = lax.axis_index("dp")
        self.z = lax.axis_index("fsdp")
        self.core = lax.rem(self.dp, 2)
        self.chip = self.dp // 2
        self.square = self.chips == 4
        if self.square:
            a, b, c = self.chip // 2, lax.rem(self.chip, 2), self.core
            self.near = lax.rem(a + 1 - c, 2) * 2 + lax.rem(b + c, 2)
            self.side = lax.rem(a + c, 2) * 2 + lax.rem(b + 1 - c, 2)
            self.far = (1 - a) * 2 + (1 - b)
            self.mates = [self.near, self.side, self.far]
        else:
            self.mates = [lax.rem(self.chip + k, self.chips) for k in range(1, self.chips)]

    def at_chip(self, chip):
        return (chip * 2 + self.core, self.z)

    def sibling(self):
        return (self.chip * 2 + 1 - self.core, self.z)

    def at_z(self, k):
        return (self.dp, lax.rem(self.z + k, self.nz))

    def z_from(self, k):
        return lax.rem(self.z + self.nz - k, self.nz)

    def greet(self, line, plane):
        bar = pltpu.get_barrier_semaphore()
        there = []
        if plane:
            there.append(self.sibling())
            there += [self.at_chip(m) for m in (self.mates[:2] if self.square else self.mates)]
        if line:
            there += [self.at_z(k) for k in range(1, self.nz)]
        for dev in there:
            pl.semaphore_signal(bar, inc=1, device_id=dev, device_id_type=MESH)
        pl.semaphore_wait(bar, len(there))


def remote(src, dst, send, recv, dev):
    return pltpu.make_async_remote_copy(
        src_ref=src, dst_ref=dst, send_sem=send, recv_sem=recv, device_id=dev, device_id_type=MESH
    )


class PlaneGather:
    def __init__(self, place, own, slot, send, recv):
        self.p, self.own, self.slot = place, own, slot
        self.send, self.recv = send, recv
        p = place
        mine = slot(p.dp)
        self.to_sib = remote(own, mine, send(0), recv(0), p.sibling())
        if p.square:
            self.first = [
                remote(own, mine, send(1), recv(1), p.at_chip(p.near)),
                remote(own, mine, send(2), recv(2), p.at_chip(p.side)),
            ]
            at = lambda m: slot(m * 2 + p.core)
            self.relay = remote(at(p.side), at(p.side), send(3), recv(3), p.at_chip(p.near))
            self.share = [
                remote(at(m), at(m), send(4 + i), recv(4 + i), p.sibling())
                for i, m in enumerate(p.mates)
            ]
        else:
            at = lambda m: slot(m * 2 + p.core)
            n = len(p.mates)
            self.first = [
                remote(own, mine, send(1 + i), recv(1 + i), p.at_chip(m)) for i, m in enumerate(p.mates)
            ]
            back = [lax.rem(p.chip + p.chips - k, p.chips) for k in range(1, p.chips)]
            self.share = [
                remote(at(m), at(m), send(1 + n + i), recv(1 + n + i), p.sibling())
                for i, m in enumerate(back)
            ]

    @staticmethod
    def sems(ndp):
        chips = ndp // 2
        return 7 if chips == 4 else 1 + 2 * (chips - 1)

    def start(self):
        for cp in self.first:
            cp.start()
        self.to_sib.start()

    def middle(self):
        if self.p.square:
            self.first[1].wait_recv()
            self.relay.start()
            self.share[1].start()
            self.first[0].wait_recv()
            self.share[0].start()
        else:
            for f, s in zip(self.first, self.share):
                f.wait_recv()
                s.start()

    def last(self):
        if self.p.square:
            self.relay.wait_recv()
            self.share[2].start()

    def finish(self):
        self.to_sib.wait()
        for s in self.share:
            s.wait()
        for f in self.first:
            f.wait_send()
        if self.p.square:
            self.relay.wait_send()


def layer_gather_kernel(ndp, nz, x_ref, g_ref, send, recv, zsend, zrecv, lsem):
    p = Place(ndp, nz)
    p.greet(True, True)
    me = p.dp * nz + p.z
    local = pltpu.make_async_copy(x_ref, g_ref.at[me], lsem)
    local.start()
    line = {
        k: remote(x_ref, g_ref.at[me], zsend.at[k], zrecv.at[k], p.at_z(k)) for k in range(1, nz)
    }

    def unit(k):
        zk = p.z_from(k)
        own = x_ref if k == 0 else g_ref.at[p.dp * nz + zk]
        return PlaneGather(
            p, own, lambda d: g_ref.at[d * nz + zk], lambda i: send.at[k, i], lambda i: recv.at[k, i]
        )

    units = [unit(k) for k in range(nz)]
    for k in range(1, nz):
        line[k].start()
    units[0].start()
    for k in range(1, nz):
        line[k].wait_recv()
        units[k].start()
        units[k - 1].middle()
        if k >= 2:
            units[k - 2].last()
    units[nz - 1].middle()
    if nz >= 2:
        units[nz - 2].last()
    units[nz - 1].last()
    for u in units:
        u.finish()
    for k in range(1, nz):
        line[k].wait_send()
    local.wait()


def layer_gather(ndp, nz, shard, cid):
    ns = PlaneGather.sems(ndp)
    return pl.pallas_call(
        partial(layer_gather_kernel, ndp, nz),
        out_shape=jax.ShapeDtypeStruct((ndp * nz,) + shard.shape, shard.dtype),
        in_specs=[ANY],
        out_specs=ANY,
        scratch_shapes=[
            pltpu.SemaphoreType.DMA((nz, ns)),
            pltpu.SemaphoreType.DMA((nz, ns)),
            pltpu.SemaphoreType.DMA((nz,)),
            pltpu.SemaphoreType.DMA((nz,)),
            pltpu.SemaphoreType.DMA,
        ],
        compiler_params=pltpu.CompilerParams(collective_id=cid, has_side_effects=True),
        name="layer_gather",
    )(shard)


HEAD_DIM = 64
EPS = 1e-6


def norm_parts(rows):
    centred = rows - jnp.mean(rows, axis=-1, keepdims=True)
    inverse = lax.rsqrt(jnp.mean(centred * centred, axis=-1, keepdims=True) + EPS)
    return centred * inverse, inverse


def dot(a, b):
    return lax.dot_general(a, b, (((1,), (0,)), ((), ())), preferred_element_type=f32)


def dot_nt(a, b):
    return lax.dot_general(a, b, (((1,), (1,)), ((), ())), preferred_element_type=f32)


def dot_tn(a, b):
    return lax.dot_general(a, b, (((0,), (0,)), ((), ())), preferred_element_type=f32)


class Exchange:
    def __init__(self, p, src, dst, send, recv):
        self.copies = []
        for k in range(1, p.nz):
            dev = p.at_z(k)
            self.copies.append(remote(src.at[dev[1]], dst.at[p.z], send.at[k], recv.at[k], dev))
        self.local = pltpu.make_async_copy(src.at[p.z], dst.at[p.z], send.at[0])

    def start(self):
        for cp in self.copies:
            cp.start()
        self.local.start()

    def wait(self):
        for cp in self.copies:
            cp.wait()
        self.local.wait()


def route(info, place_ref, image, cap, slots, experts):
    cols = jnp.transpose(info)
    rank_c, one_c, two_c = cols[:, 0:1], cols[:, 1:2], cols[:, 2:3]
    rank_r, one_r, two_r = info[0:1, :], info[1:2, :], info[2:3, :]
    lanes = info.shape[1]
    earlier = rank_c < rank_r
    count = lambda m: jnp.sum(jnp.where(m, 1.0, 0.0), axis=0, keepdims=True)
    pos_one = count(earlier & (one_c == one_r))
    pos_two = count(earlier & (two_c == two_r)) + count(one_c == two_r)
    code = lambda pos, pick: jnp.where(
        (pos < cap) & (pick >= 0), pick * slots + (pos + image * cap), -1.0
    ).astype(jnp.int32)
    code_one, code_two = code(pos_one, one_r), code(pos_two, two_r)
    for e in range(experts):
        slot = lax.broadcasted_iota(jnp.int32, (slots, lanes), 0) + e * slots
        hit = (slot == code_one) | (slot == code_two)
        place_ref[e * slots : (e + 1) * slots, image * lanes : (image + 1) * lanes] = jnp.where(
            hit, 1.0, 0.0
        ).astype(bf16)


def attend_kernel(
    ndp, nz, cap, seq, experts, images,
    x_ref, dy_ref, info_ref, gain_ref, wqkv_ref, wout_ref, win_ref, wback_ref,
    wi_ref, wb_ref, rtok_ref, rdy_ref, place_ref, mixed_ref, probs_ref, att_ref, res_ref,
    tok_ref, stok_ref, sdy_ref, gsend, grecv, tsend, trecv, ysend, yrecv, lsem,
):
    p = Place(ndp, nz)
    rows, d = x_ref.shape[1], x_ref.shape[2]
    lanes = info_ref.shape[2]
    slots = stok_ref.shape[1]
    pairs = d // 128
    p.greet(True, True)
    units, locals_ = [], []
    for t in range(win_ref.shape[0]):
        for w, (own, full) in enumerate(((win_ref, wi_ref), (wback_ref, wb_ref))):
            n = t * 2 + w
            units.append(
                PlaneGather(
                    p, own.at[t], lambda dd, full=full, t=t: full.at[t, dd],
                    lambda i, n=n: gsend.at[n, i], lambda i, n=n: grecv.at[n, i],
                )
            )
            locals_.append(pltpu.make_async_copy(own.at[t], full.at[t, p.dp], lsem.at[n]))
    for u, lc in zip(units, locals_):
        u.start()
        lc.start()

    tok_ref[...] = jnp.zeros_like(tok_ref)
    for i in range(images):
        route(info_ref[i], place_ref, i, cap, slots, experts)
        tok_ref[i * lanes : i * lanes + rows, :] = dy_ref[i]

    def dispatch(out_ref):
        @pl.loop(0, experts)
        def _(e):
            out_ref[e] = dot(
                place_ref[pl.ds(pl.multiple_of(e * slots, slots), slots), :], tok_ref[...]
            ).astype(bf16)

    dispatch(sdy_ref)
    send_dy = Exchange(p, sdy_ref, rdy_ref, ysend, yrecv)
    send_dy.start()

    gain_one, gain_two = gain_ref[0:1, :], gain_ref[1:2, :]
    if mixed_ref.shape[1] > rows:
        for i in range(images):
            mixed_ref[i, rows:, :] = jnp.zeros((mixed_ref.shape[1] - rows, 3 * d), bf16)

    @pl.loop(0, images)
    def _(i):
        normed, _inv = norm_parts(x_ref[i].astype(f32))
        first = (normed * gain_one).astype(bf16)
        for part in range(3):
            mixed_ref[i, :rows, part * d : (part + 1) * d] = dot(
                first, wqkv_ref[:, part * d : (part + 1) * d]
            ).astype(bf16)

    low_half = lax.broadcasted_iota(jnp.int32, (1, 128), 1) < HEAD_DIM
    valid = lax.broadcasted_iota(jnp.int32, (1, lanes), 1) < seq

    @pl.loop(0, images * pairs)
    def _(n):
        i = n // pairs
        at = lambda part: pl.ds(pl.multiple_of(part * d + (n - i * pairs) * 128, 128), 128)
        q, k, v = mixed_ref[i, :rows, at(0)], mixed_ref[i, :, at(1)], mixed_ref[i, :, at(2)]
        got = []
        for h in range(2):
            mask = low_half if h == 0 else ~low_half
            scores = dot_nt(jnp.where(mask, q, jnp.zeros_like(q)), k) * HEAD_DIM**-0.5
            scores = jnp.where(valid, scores, -1e30)
            e = jnp.exp(scores - jnp.max(scores, axis=-1, keepdims=True))
            prob = (e / jnp.sum(e, axis=-1, keepdims=True)).astype(bf16)
            probs_ref[n * 2 + h] = prob
            got.append(dot(prob, v))
        att_ref[i, :, at(0)] = jnp.where(low_half, got[0], got[1]).astype(bf16)

    @pl.loop(0, images)
    def _(i):
        residual = x_ref[i].astype(f32) + dot(att_ref[i], wout_ref[...])
        res_ref[i] = residual
        normed, _inv = norm_parts(residual)
        tok_ref[pl.ds(pl.multiple_of(i * lanes, lanes), rows), :] = (normed * gain_two).astype(bf16)

    dispatch(stok_ref)
    send_tok = Exchange(p, stok_ref, rtok_ref, tsend, trecv)
    send_tok.start()
    for u in units:
        u.middle()
    for u in units:
        u.last()
    for u, lc in zip(units, locals_):
        u.finish()
        lc.wait()
    send_dy.wait()
    send_tok.wait()


def attend(ndp, nz, cap, slots, seq, experts, cid, x, dy, info, gain, wqkv, wout, win, wback):
    images, rows, d = x.shape
    lanes = info.shape[2]
    tiles = win.shape[0]
    ns = PlaneGather.sems(ndp)
    shape = jax.ShapeDtypeStruct
    dma = pltpu.SemaphoreType.DMA
    return pl.pallas_call(
        partial(attend_kernel, ndp, nz, cap, seq, experts, images),
        out_shape=(
            shape((tiles, ndp) + win.shape[1:], bf16),
            shape((tiles, ndp) + wback.shape[1:], bf16),
            shape((nz, slots, d), bf16),
            shape((nz, slots, d), bf16),
            shape((experts * slots, images * lanes), bf16),
            shape((images, lanes, 3 * d), bf16),
            shape((images * d // HEAD_DIM, rows, lanes), bf16),
            shape((images, rows, d), bf16),
            shape((images, rows, d), f32),
        ),
        in_specs=[VM] * 6 + [ANY] * 2,
        out_specs=(ANY,) * 4 + (VM,) * 5,
        scratch_shapes=[
            pltpu.VMEM((images * lanes, d), bf16),
            pltpu.VMEM((experts, slots, d), bf16),
            pltpu.VMEM((experts, slots, d), bf16),
            dma((2 * tiles, ns)), dma((2 * tiles, ns)),
            dma((nz,)), dma((nz,)), dma((nz,)), dma((nz,)),
            dma((2 * tiles,)),
        ],
        compiler_params=pltpu.CompilerParams(
            collective_id=cid, has_side_effects=True, vmem_limit_bytes=60 << 20
        ),
        name="attend",
    )(x, dy, info, gain, wqkv, wout, win, wback)


class PlaneScatter:
    def __init__(self, place, part, sib, got, out, send, recv):
        self.p, self.part, self.sib, self.got, self.out = place, part, sib, got, out
        p = place
        self.pair = remote(part.at[:, 1 - p.core], sib, send(0), recv(0), p.sibling())
        at = lambda m: part.at[m, p.core]
        if p.square:
            self.first = [
                remote(at(p.far), got.at[0], send(1), recv(1), p.at_chip(p.near)),
                remote(at(p.near), got.at[1], send(2), recv(2), p.at_chip(p.near)),
            ]
            self.second = remote(at(p.side), got.at[2], send(3), recv(3), p.at_chip(p.side))
        else:
            self.first = [
                remote(at(m), got.at[i], send(1 + i), recv(1 + i), p.at_chip(m))
                for i, m in enumerate(p.mates)
            ]

    @staticmethod
    def sems(ndp):
        chips = ndp // 2
        return 4 if chips == 4 else chips

    @staticmethod
    def blocks(ndp):
        return ndp // 2 - 1

    def add(self, m, more):
        here = self.part.at[m, self.p.core]
        here[...] = (here[...].astype(f32) + more.astype(f32)).astype(here.dtype)

    def start(self):
        self.pair.start()

    def middle(self):
        p = self.p
        self.pair.wait_recv()
        if p.square:
            self.add(p.far, self.sib[p.far])
            self.first[0].start()
            self.add(p.near, self.sib[p.near])
            self.first[1].start()
            self.add(p.side, self.sib[p.side])
        else:
            for m, cp in zip(p.mates, self.first):
                self.add(m, self.sib[m])
                cp.start()

    def last(self):
        if self.p.square:
            self.first[0].wait_recv()
            self.add(self.p.side, self.got[0])
            self.second.start()

    def finish(self):
        p = self.p
        total = self.part[p.chip, p.core].astype(f32) + self.sib[p.chip].astype(f32)
        if p.square:
            self.first[1].wait_recv()
            total += self.got[1].astype(f32)
            self.second.wait_recv()
            total += self.got[2].astype(f32)
        else:
            for i, cp in enumerate(self.first):
                cp.wait_recv()
                total += self.got[i].astype(f32)
        self.out[...] = total
        for cp in [self.pair] + self.first + ([self.second] if p.square else []):
            cp.wait_send()


def expert_kernel(
    ndp, nz, experts,
    wi_ref, wb_ref, buf_ref, dy_ref, wr_ref,
    rgrad_ref, eo_ref, gi_ref, gb_ref, gr_ref,
    gs_ref, buft_ref, act_ref, gh_ref, oacc_ref, gacc_ref, pin_ref, pback_ref,
    sin_ref, sback_ref, xin_ref, xback_ref, sgrad_ref, rp_ref,
    ssend, srecv, esend, erecv,
):
    p = Place(ndp, nz)
    tiles, d, width = wi_ref.shape
    slots = buf_ref.shape[1]
    rows = nz * slots
    p.greet(True, True)

    lane = lax.broadcasted_iota(jnp.int32, (1, 128), 1)

    @pl.loop(0, nz)
    def _(s):
        logits = dot(buf_ref[s], wr_ref[...])
        logits = jnp.where(lane < experts, logits, -1e30)
        ex = jnp.exp(logits - jnp.max(logits, axis=-1, keepdims=True))
        rp = ex / jnp.sum(ex, axis=-1, keepdims=True)
        rp_ref[s] = rp
        gate = jnp.sum(jnp.where(lane == p.z, rp, 0.0), axis=-1, keepdims=True)
        gs_ref[s] = (gate * dy_ref[s].astype(f32)).astype(bf16)

    buft_ref[...] = jnp.transpose(buf_ref[...].reshape(rows, d))

    scatters = []
    for t in range(tiles):
        for w, (part, sib, got, out) in enumerate(
            ((pin_ref, sin_ref, xin_ref, gi_ref), (pback_ref, sback_ref, xback_ref, gb_ref))
        ):
            n = t * 2 + w
            scatters.append(
                PlaneScatter(
                    p, part.at[t], sib.at[t], got.at[t], out.at[t],
                    lambda i, n=n: ssend.at[n, i], lambda i, n=n: srecv.at[n, i],
                )
            )
    both = lambda t: scatters[2 * t : 2 * t + 2]

    step = min(256, width)
    per_in, per_back = d // ndp, width // ndp

    for t in range(tiles):

        @pl.loop(0, nz * (width // step))
        def _(n):
            s = n // (width // step)
            cols = pl.ds(pl.multiple_of((n - s * (width // step)) * step, step), step)
            h = dot(buf_ref[s], wi_ref[t, :, cols])
            grad = dot_nt(gs_ref[s], wb_ref[t, cols, :])
            k0, k1 = 0.7978845608028654, 0.044715 * 0.7978845608028654
            h2 = h * h
            th = jnp.tanh(h * (k0 + k1 * h2))
            half = 0.5 * (1.0 + th)
            act_ref[s, :, cols] = (h * half).astype(bf16)
            slope = half + 0.5 * h * (1.0 - th * th) * (k0 + 3.0 * k1 * h2)
            gh_ref[s, :, cols] = (grad * slope).astype(bf16)

        @pl.loop(0, nz)
        def _(s):
            o = dot(act_ref[s], wb_ref[t])
            g = dot_nt(gh_ref[s], wi_ref[t])
            if t == 0:
                oacc_ref[s] = o
                gacc_ref[s] = g
            else:
                oacc_ref[s] += o
                gacc_ref[s] += g

        @pl.loop(0, width // step)
        def _(n):
            cols = pl.ds(pl.multiple_of(n * step, step), step)
            got = dot(buft_ref[...], gh_ref[:, :, cols].reshape(rows, step)).astype(bf16)
            pin_ref[t, :, :, :, cols] = got.reshape(ndp // 2, 2, per_in, step)
            gotb = dot_tn(
                act_ref[:, :, cols].reshape(rows, step), gs_ref[...].reshape(rows, d)
            ).astype(bf16)
            many = step // per_back // 2
            pback_ref[t, pl.ds(n * many, many)] = gotb.reshape(many, 2, per_back, d)

        if t >= 2:
            for u in both(t - 2):
                u.last()
        if t >= 1:
            for u in both(t - 1):
                u.middle()
        for u in both(t):
            u.start()

    gr_ref[...] = jnp.zeros_like(gr_ref)

    @pl.loop(0, nz)
    def _(s):
        out = oacc_ref[s].astype(bf16)
        eo_ref[s] = out
        rp = rp_ref[s]
        mine = jnp.where(lane == p.z, 1.0, 0.0)
        gate = jnp.sum(mine * rp, axis=-1, keepdims=True)
        ggate = jnp.sum(out.astype(f32) * dy_ref[s].astype(f32), axis=-1, keepdims=True)
        contrib = (ggate * gate) * (mine - rp)
        hi = contrib.astype(bf16)
        lo = (contrib - hi.astype(f32)).astype(bf16)
        sgrad_ref[s] = (gacc_ref[s] + dot_nt(hi, wr_ref[...]) + dot_nt(lo, wr_ref[...])).astype(bf16)
        gr_ref[...] += dot_tn(buf_ref[s], hi) + dot_tn(buf_ref[s], lo)

    back = Exchange(p, sgrad_ref, rgrad_ref, esend, erecv)
    back.start()
    for u in both(tiles - 2):
        u.last()
    for u in both(tiles - 1):
        u.middle()
    for u in both(tiles - 1):
        u.last()
    for u in scatters:
        u.finish()
    back.wait()


def expert(ndp, nz, experts, cid, wi, wb, buf, dy, wr):
    tiles, d, width = wi.shape
    slots = buf.shape[1]
    rows = nz * slots
    per_in, per_back = d // ndp, width // ndp
    chips = ndp // 2
    shape = jax.ShapeDtypeStruct
    dma = pltpu.SemaphoreType.DMA
    nb = PlaneScatter.blocks(ndp)
    return pl.pallas_call(
        partial(expert_kernel, ndp, nz, experts),
        out_shape=(
            shape((nz, slots, d), bf16),
            shape((nz, slots, d), bf16),
            shape((tiles, per_in, width), f32),
            shape((tiles, per_back, d), f32),
            shape((d, 128), f32),
        ),
        in_specs=[VM] * 5,
        out_specs=(ANY, VM, VM, VM, VM),
        scratch_shapes=[
            pltpu.VMEM((nz, slots, d), bf16),
            pltpu.VMEM((d, rows), bf16),
            pltpu.VMEM((nz, slots, width), bf16),
            pltpu.VMEM((nz, slots, width), bf16),
            pltpu.VMEM((nz, slots, d), f32),
            pltpu.VMEM((nz, slots, d), f32),
            pltpu.VMEM((tiles, chips, 2, per_in, width), bf16),
            pltpu.VMEM((tiles, chips, 2, per_back, d), bf16),
            pltpu.VMEM((tiles, chips, per_in, width), bf16),
            pltpu.VMEM((tiles, chips, per_back, d), bf16),
            pltpu.VMEM((tiles, nb, per_in, width), bf16),
            pltpu.VMEM((tiles, nb, per_back, d), bf16),
            pltpu.VMEM((nz, slots, d), bf16),
            pltpu.VMEM((nz, slots, 128), f32),
            dma((2 * tiles, PlaneScatter.sems(ndp))), dma((2 * tiles, PlaneScatter.sems(ndp))),
            dma((nz,)), dma((nz,)),
        ],
        compiler_params=pltpu.CompilerParams(
            collective_id=cid, has_side_effects=True, vmem_limit_bytes=62 << 20
        ),
        name="expert",
    )(wi, wb, buf, dy, wr)


def norm_back(grad, normed, inverse):
    first = jnp.mean(grad, axis=-1, keepdims=True)
    second = normed * jnp.mean(grad * normed, axis=-1, keepdims=True)
    return inverse * (grad - first - second)


class LineScatter:
    def __init__(self, place, total, sent, got, out, send, recv):
        self.p, self.total, self.sent, self.got, self.out = place, total, sent, got, out
        self.copies = []
        for k in range(1, place.nz):
            dev = place.at_z(k)
            self.copies.append(
                remote(sent.at[dev[1]], got.at[place.z], send(k), recv(k), dev)
            )

    def start(self):
        count = self.out.shape[0]
        for k in range(self.p.nz):
            self.sent[k, :count, :] = self.total[k * count : (k + 1) * count, :].astype(
                self.sent.dtype
            )
        for cp in self.copies:
            cp.start()

    def finish(self):
        p, count = self.p, self.out.shape[0]
        for cp in self.copies:
            cp.wait()
        total = self.sent[p.z].astype(f32)
        for k in range(1, p.nz):
            total += self.got[p.z_from(k)].astype(f32)
        self.out[...] = total[:count]


def back_kernel(
    ndp, nz, experts,
    rg_ref, eo_ref, place_ref, x_ref, dy_ref, mixed_ref, probs_ref, att_ref, res_ref,
    gain_ref, wqkv_ref, wout_ref, wr_ref, gr_ref,
    out_ref, gin_ref, gl_ref, gsm_ref,
    ro_ref, gres_ref, branch_ref, gatt_ref, gmix_ref, first_ref, vec_ref,
    part_ref, sib_ref, got_ref, tot_ref, psm_ref, ssm_ref, xsm_ref, tsm_ref,
    zsent_ref, zgot_ref, zssm_ref, zgsm_ref,
    ysend, yrecv, ssend, srecv, zsend, zrecv,
):
    p = Place(ndp, nz)
    images, rows, d = x_ref.shape
    lanes = place_ref.shape[1] // images
    slots = rg_ref.shape[0] // experts
    pairs = d // 128
    chips, per = ndp // 2, d // ndp
    p.greet(True, True)
    outs = Exchange(p, eo_ref, ro_ref, ysend, yrecv)
    outs.start()

    scatters, lines = [], []
    for n in range(5):
        part, sib, got, tot, zs, zg, out = (
            (part_ref.at[n], sib_ref.at[n], got_ref.at[n], tot_ref.at[n],
             zsent_ref.at[n], zgot_ref.at[n], gl_ref.at[n])
            if n < 4
            else (psm_ref, ssm_ref, xsm_ref, tsm_ref, zssm_ref, zgsm_ref, gsm_ref)
        )
        scatters.append(
            PlaneScatter(p, part, sib, got, tot, lambda i, n=n: ssend.at[n, i], lambda i, n=n: srecv.at[n, i])
        )
        lines.append(
            LineScatter(p, tot, zs, zg, out, lambda i, n=n: zsend.at[n, i], lambda i, n=n: zrecv.at[n, i])
        )

    gain_one, gain_two = gain_ref[0:1, :], gain_ref[1:2, :]
    vec_ref[...] = jnp.zeros_like(vec_ref)

    @pl.loop(0, images)
    def _(i):
        hits = place_ref[:, pl.ds(pl.multiple_of(i * lanes, lanes), lanes)]
        grad_second = dot_tn(hits, rg_ref[...])[:rows]
        normed, inverse = norm_parts(res_ref[i])
        vec_ref[1:2, :] += jnp.sum(grad_second * normed, axis=0, keepdims=True)
        grad = dy_ref[i].astype(f32) + norm_back(grad_second * gain_two, normed, inverse)
        gres_ref[i] = grad
        branch = grad.astype(bf16)
        branch_ref[i] = branch
        gatt_ref[i] = dot_nt(branch, wout_ref[...]).astype(bf16)
        normed_one, _inv = norm_parts(x_ref[i].astype(f32))
        first_ref[i] = (normed_one * gain_one).astype(bf16)

    part_ref[3] = (
        dot_tn(att_ref[...].reshape(images * rows, d), branch_ref[...].reshape(images * rows, d))
        .astype(bf16)
        .reshape(chips, 2, per, d)
    )
    scatters[3].start()

    low_half = lax.broadcasted_iota(jnp.int32, (1, 128), 1) < HEAD_DIM
    scale = HEAD_DIM**-0.5

    @pl.loop(0, images * pairs)
    def _(n):
        i = n // pairs
        at = lambda part: pl.ds(pl.multiple_of(part * d + (n - i * pairs) * 128, 128), 128)
        q, k, v = mixed_ref[i, :rows, at(0)], mixed_ref[i, :, at(1)], mixed_ref[i, :, at(2)]
        ga = gatt_ref[i, :, at(0)]
        gq, gk, gv = [], [], []
        for h in range(2):
            mask = low_half if h == 0 else ~low_half
            prob = probs_ref[n * 2 + h]
            gv.append(dot_tn(prob, ga)[:rows])
            weighting = dot_nt(jnp.where(mask, ga, jnp.zeros_like(ga)), v)
            wide = prob.astype(f32)
            scores = wide * (weighting - jnp.sum(wide * weighting, axis=-1, keepdims=True))
            scores = scores.astype(bf16)
            gq.append(dot(scores, k))
            gk.append(dot_tn(scores, q)[:rows])
        pick = lambda pair, by: jnp.where(low_half, pair[0], pair[1]) * by
        gmix_ref[i, :, at(0)] = pick(gq, scale).astype(bf16)
        gmix_ref[i, :, at(1)] = pick(gk, scale).astype(bf16)
        gmix_ref[i, :, at(2)] = pick(gv, 1.0).astype(bf16)

    scatters[3].middle()
    for n in range(3):
        part_ref[n] = (
            dot_tn(
                first_ref[...].reshape(images * rows, d),
                gmix_ref[:, :, n * d : (n + 1) * d].reshape(images * rows, d),
            )
            .astype(bf16)
            .reshape(chips, 2, per, d)
        )
        scatters[n].start()

    scatters[3].last()

    @pl.loop(0, images)
    def _(i):
        grad_first = dot_nt(gmix_ref[i], wqkv_ref[...])
        normed, inverse = norm_parts(x_ref[i].astype(f32))
        vec_ref[0:1, :] += jnp.sum(grad_first * normed, axis=0, keepdims=True)
        gin_ref[i] = gres_ref[i] + norm_back(grad_first * gain_one, normed, inverse)

    lane = lax.broadcasted_iota(jnp.int32, (1, 128), 1)
    cols = jnp.transpose(vec_ref[...])
    small = jnp.where(
        lane == experts, cols[:, 0:1], jnp.where(lane == experts + 1, cols[:, 1:2], gr_ref[...])
    )
    psm_ref[...] = small.reshape(chips, 2, per, 128)
    scatters[4].start()
    order = (0, 1, 2, 4)
    for n in order:
        scatters[n].middle()
    scatters[3].finish()
    lines[3].start()
    for n in order:
        scatters[n].last()
    outs.wait()

    @pl.loop(0, images)
    def _(i):
        normed, _inv = norm_parts(res_ref[i])
        logits = dot((normed * gain_two).astype(bf16), wr_ref[...])
        logits = jnp.where(lane < experts, logits, -1e30)
        ex = jnp.exp(logits - jnp.max(logits, axis=-1, keepdims=True))
        rp = ex / jnp.sum(ex, axis=-1, keepdims=True)
        total = res_ref[i]
        for e in range(experts):
            hits = place_ref[e * slots : (e + 1) * slots, pl.ds(pl.multiple_of(i * lanes, lanes), lanes)]
            gate = jnp.sum(jnp.where(lane == e, rp, 0.0), axis=-1, keepdims=True)
            total = total + gate * dot_tn(hits, ro_ref[e])[:rows]
        out_ref[i] = total.astype(bf16)

    for n in order:
        scatters[n].finish()
        lines[n].start()
    for n in (3,) + order:
        lines[n].finish()


def back(ndp, nz, experts, cid, rgrad, eo, place, x, dy, mixed, probs, att, res, gain, wqkv, wout, wr, gr):
    images, rows, d = x.shape
    lanes = place.shape[1] // images
    chips, per = ndp // 2, d // ndp
    group = per // nz
    tall, short = -(-group // 16) * 16, -(-group // 8) * 8
    nb = PlaneScatter.blocks(ndp)
    slots = rgrad.shape[1]
    shape = jax.ShapeDtypeStruct
    dma = pltpu.SemaphoreType.DMA
    vm = pltpu.VMEM
    ns = PlaneScatter.sems(ndp)
    return pl.pallas_call(
        partial(back_kernel, ndp, nz, experts),
        out_shape=(
            shape((images, rows, d), bf16),
            shape((images, rows, d), f32),
            shape((4, group, d), f32),
            shape((group, 128), f32),
        ),
        in_specs=[VM, ANY] + [VM] * 12,
        out_specs=(VM,) * 4,
        scratch_shapes=[
            vm((nz, slots, d), bf16),
            vm((images, rows, d), f32),
            vm((images, rows, d), bf16),
            vm((images, rows, d), bf16),
            vm((images, rows, 3 * d), bf16),
            vm((images, rows, d), bf16),
            vm((8, d), f32),
            vm((4, chips, 2, per, d), bf16),
            vm((4, chips, per, d), bf16),
            vm((4, nb, per, d), bf16),
            vm((4, per, d), f32),
            vm((chips, 2, per, 128), f32),
            vm((chips, per, 128), f32),
            vm((nb, per, 128), f32),
            vm((per, 128), f32),
            vm((4, nz, tall, d), bf16),
            vm((4, nz, tall, d), bf16),
            vm((nz, short, 128), f32),
            vm((nz, short, 128), f32),
            dma((nz,)), dma((nz,)),
            dma((5, ns)), dma((5, ns)),
            dma((5, nz)), dma((5, nz)),
        ],
        compiler_params=pltpu.CompilerParams(
            collective_id=cid, has_side_effects=True, vmem_limit_bytes=62 << 20
        ),
        name="back",
    )(rgrad.reshape(experts * slots, d), eo, place, x, dy, mixed, probs, att, res, gain, wqkv, wout, wr, gr)


def up(value, unit):
    return -(-value // unit) * unit


def per_device(ndp, nz, images, gain_one, w_qkv, w_out, gain_two, w_router, w_in, w_back, choices, priority, cotangent):
    count, seq, d = images.shape
    experts, ff = w_router.shape[1], w_in.shape[2]
    devices = ndp * nz
    group = d // devices
    cap = (42 * seq + 20 * experts - 1) // (20 * experts)
    slots = up(count * cap, 16)
    rows, lanes = up(seq, 16), up(seq, 128)
    tiles = 3
    chunk = ff // ndp // tiles

    fold = 16 // math.gcd(group, 16)
    thin = 4 * d // fold
    small = jnp.concatenate([gain_one[:, None], gain_two[:, None], w_router], axis=1)
    flat = jnp.pad(small.reshape(-1), (0, group * fold * 128 - small.size)).reshape(group * fold, 128)
    main = jnp.concatenate([w_qkv, w_out], axis=1)
    main = main.reshape(group, fold, thin).transpose(1, 0, 2).reshape(group * fold, thin)
    layers = layer_gather(ndp, nz, jnp.concatenate([main, flat], axis=1), 0)
    main = layers[:, :, :thin].reshape(devices, fold, group, thin).transpose(0, 2, 1, 3).reshape(d, 4 * d)
    wqkv, wout = main[:, : 3 * d], main[:, 3 * d :]
    small = layers[:, :, thin:].reshape(devices, -1)[:, : group * (2 + experts)].reshape(d, 2 + experts)
    gain = jnp.pad(small[:, :2].astype(f32).T, ((0, 6), (0, 0)))
    wr = jnp.pad(small[:, 2:], ((0, 0), (0, 128 - experts)))

    x = jnp.pad(images, ((0, 0), (0, rows - seq), (0, 0)))
    dy = jnp.pad(cotangent, ((0, 0), (0, rows - seq), (0, 0)))
    info = jnp.stack([priority, choices[:, :, 0], choices[:, :, 1]], axis=1).astype(f32)
    info = jnp.concatenate(
        [
            jnp.pad(info[:, :1], ((0, 0), (0, 0), (0, lanes - seq)), constant_values=1e6),
            jnp.pad(info[:, 1:2], ((0, 0), (0, 0), (0, lanes - seq)), constant_values=-1.0),
            jnp.pad(info[:, 2:], ((0, 0), (0, 0), (0, lanes - seq)), constant_values=-2.0),
            jnp.zeros((count, 5, lanes), f32),
        ],
        axis=1,
    )
    win = w_in[0].reshape(d // ndp, ndp, tiles, chunk).transpose(2, 0, 1, 3).reshape(tiles, d // ndp, ndp * chunk)
    wback = w_back[0].reshape(tiles, chunk, d)
    wi, wb, rtok, rdy, place, mixed, probs, att, res = attend(
        ndp, nz, cap, slots, seq, experts, 1, x, dy, info, gain, wqkv, wout, win, wback
    )
    rgrad, eo, gi, gb, gr = expert(
        ndp, nz, experts, 2,
        wi.reshape(tiles, d, ndp * chunk), wb.reshape(tiles, ndp * chunk, d), rtok, rdy, wr,
    )
    out, gin, gl, gsm = back(
        ndp, nz, experts, 3, rgrad, eo, place, x, dy, mixed, probs, att, res, gain, wqkv, wout, wr, gr
    )
    grad_qkv = jnp.concatenate([gl[0], gl[1], gl[2]], axis=1)
    grad_in = gi.reshape(tiles, d // ndp, ndp, chunk).transpose(1, 2, 0, 3).reshape(1, d // ndp, ff)
    return (
        out[:, :seq], gin[:, :seq], gsm[:, experts], grad_qkv, gl[3], gsm[:, experts + 1], gsm[:, :experts],
        grad_in, gb.reshape(1, ff // ndp, d),
    )


def solution(mesh):
    ndp, nz = mesh.shape["dp"], mesh.shape["fsdp"]
    both = ("dp", "fsdp")
    tokens, rows, expert_rows = P(both, None, None), P(both, None), P("fsdp", "dp", None)
    return jax.shard_map(
        partial(per_device, ndp, nz),
        mesh=mesh,
        in_specs=(tokens, P(both), rows, rows, P(both), rows, expert_rows, expert_rows, tokens, rows, tokens),
        out_specs=(tokens, tokens, P(both), rows, rows, P(both), rows, expert_rows, expert_rows),
        check_vma=False,
    )
```

time: 709 us -> 304 us (0.43)
  Pallas kernels: 0 us -> 255 us
  waiting for transfers between devices: 227 us -> 0 us
  blocking collectives: 149 us -> 0 us
  matrix products: 137 us -> 0 us
  local copies, waits for them, and re-layouts: 92.2 us -> 43.4 us
  other arithmetic: 46.8 us -> 4.39 us
  starting transfers between devices: 34.1 us -> 0 us
  between operations: 16.1 us -> 0.83 us
    pallas_call x0 -> x4, Pallas kernels: none -> 255 us  [the longest x1 93.2 us: expert(): pl.pallas_call(partial(expert_kernel, ndp, nz, experts), out_shape=(shape...]
    reduce_scatter x4 -> x0, waiting for transfers between devices: 170 us -> none  [the longest x1 125 us: per_device(): lax.psum_scatter(total_qkv, ('dp', 'fsdp'), scatter_dimension=0, tiled=True)]
    dot_general x42 -> x0, matrix products: 137 us -> none  [the longest x2 16.4 us: per_device(): jnp.einsum('secd,efd->secf', arrived_grouped, full_back, preferred_elemen...]
    unnamed x2 -> x0, blocking collectives: 82.2 us -> none
    all_gather x1 -> x0, blocking collectives: 66.6 us -> none  [fetch_weights(): lax.all_gather(w_router, ('dp', 'fsdp'), axis=0, tiled=True)]
    all_to_all x8 -> x0, waiting for transfers between devices: 35.3 us -> none  [the longest x2 14 us: per_device(): lax.all_to_all(grad_sent, 'fsdp', split_axis=0, concat_axis=0, tiled=True)]
    all_to_all x8 -> x0, starting transfers between devices: 33.2 us -> none  [the longest x2 8.77 us: per_device(): lax.all_to_all(grad_sent, 'fsdp', split_axis=0, concat_axis=0, tiled=True)]
    reduce_sum x22 -> x0, other arithmetic: 21.1 us -> none  [the longest x2 9.72 us: per_device(): grad_gates = jnp.sum(upstream[:, None, :] * picked, axis=2)]
  transfers between devices with their start and end apart: 16 -> 0, of which waited for: 10 -> 0; matrix products, arithmetic and copies ran while one was open for 29% -> 0% of each run, Pallas kernels for 0% -> 0%
where the time goes in v1:
time: 304 us; the launch traced here: 303 us
  Pallas kernels  255 us (84%)
  local copies, waits for them, and re-layouts  43.4 us (14%)
  other arithmetic  4.39 us (1%)
    pallas_call x1, Pallas kernels, expert(): pl.pallas_call(partial(expert_kernel, ndp, nz, experts), out_shape=(shape...  93.2 us
    pallas_call x1, Pallas kernels, attend(): pl.pallas_call(partial(attend_kernel, ndp, nz, cap, seq, experts, images)...  63.9 us
    pallas_call x1, Pallas kernels, back(): pl.pallas_call(partial(back_kernel, ndp, nz, experts), out_shape=(shape((...  63 us
    pallas_call x1, Pallas kernels, layer_gather(): pl.pallas_call(partial(layer_gather_kernel, ndp, nz), out_shape=jax.Shape...  34.5 us
    unnamed x26, local copies, waits for them, and re-layouts  11.5 us
    reshape x1, local copies, waits for them, and re-layouts, per_device(): layers[:, :, :thin].reshape(devices, fold, group, thin)  9.25 us
    slice x2, local copies, waits for them, and re-layouts, per_device(): wqkv, wout = (main[:, :3 * d], main[:, 3 * d:])  6.44 us

profile of v1, /device:TPU:0, one launch (start us, length us, event | category | flops | bytes accessed | tf_op | source)
XLA Modules:
  0.0 303.2 jit_solution(17310585523974372716)
XLA Ops:
  0.7 0.8 pad_maximum_fusion.3
  2.4 0.8 slice_bitcast_fusion.5
  3.9 0.9 pad_maximum_fusion.2
  5.6 0.9 pad.31.x_ref
  6.8 0.9 pad.32.dy_ref
  7.9 0.9 reshape_squeeze.6
  8.8 1.1 reshape.71.win_ref
  9.9 34.5 %layer_gather.1 = bf16[32,48,1664]{2,1,0:T(8,128)(2,1)} custom-call(bf16[48,1664]{1,0:T(8,128)(2,1)} %pad_maximum_fusion.1.x_ref), custom_call_target="tpu_custom_call" | custom-call | tf_op jit(solution)/shard_map/layer_gather/pallas_call | solution.py:173
  44.4 4.8 %slice.71 = bf16[32,48,1536]{2,1,0:T(8,128)(2,1)} slice(bf16[32,48,1664]{2,1,0:T(8,128)(2,1)} %layer_gather.1), slice={[0:32], [0:48], [0:1536]} | slice | bytes 9437184 | tf_op jit(solution)/shard_map/slice | solution.py:875
  49.2 9.2 %copy.36 = bf16[32,2,24,1536]{3,1,2,0:T(2,128)(2,1)} copy(bf16[32,2,24,1536]{3,2,1,0:T(8,128)(2,1)} %bitcast.53) | data formatting | bytes 9437184 | tf_op jit(solution)/shard_map/reshape | solution.py:875
  58.5 5.8 %copy.45 = bf16[96,8,2,1536]{3,1,2,0:T(8,128)(2,1)} copy(bf16[96,8,2,1536]{3,2,1,0:T(2,128)(2,1)} %bitcast.54) | data formatting | bytes 9437184
  65.5 0.7 pad.39.wr_ref
  66.2 2.4 slice.87.wout_ref
  68.5 4.1 %slice.86.wqkv_ref = bf16[768,2304]{1,0:T(8,128)(2,1)} slice(bf16[768,3072]{1,0:T(8,128)(2,1)} %bitcast.52), slice={[0:768], [0:2304]} | slice | bytes 7077888 | tf_op jit(solution)/shard_map/slice | solution.py:876
  72.6 63.9 %attend.1 = (bf16[3,8,96,1024]{3,2,1,0:T(8,128)(2,1)}, bf16[3,8,128,768]{3,2,1,0:T(8,128)(2,1)}, bf16[4,208,768]{2,1,0:T(8,128)(2,1)}, bf16[4,208,768]{2,1,0:T(8...) custom-call(bf16[2,208,768]{2,1,0:T(8,128)(2,1)} %pad.31.x_ref, ...), custom_call_target="tpu_custom_call" | custom-call | tf_op jit(solution)/shard_map/attend/pallas_call | solution.py:356
  136.5 93.2 %expert.1 = (bf16[4,208,768]{2,1,0:T(8,128)(2,1)}, bf16[4,208,768]{2,1,0:T(8,128)(2,1)}, f32[3,96,1024]{2,1,0:T(8,128)}, f32[3,128,768]{2,1,0:T(8,128)}, f32[768,128]{1,0:T(8,128)}) custom-call(bf16[3,768,1024]{2,1,0:T(8,128)(2,1)} %bitcast.57, bf16[3,1024,768]{2,1,0:T(8,128)(2,1)} %bitcast.58, bf16[4,208,768]{2,1,0:T(8,128)(2,1)} %get-tuple-element.29.buf_ref, ...), custom_call_target="tpu_custom_call" | custom-call | tf_op jit(solution)/shard_map/expert/pallas_call | solution.py:587
  229.7 63.0 %back.1 = (bf16[2,208,768]{2,1,0:T(8,128)(2,1)}, f32[2,208,768]{2,1,0:T(8,128)}, f32[4,24,768]{2,1,0:T(8,128)}, f32[24,128]{1,0:T(8,128)}) custom-call(bf16[832,768]{1,0:T(8,128)(2,1)} %bitcast.61, bf16[4,208,768]{2,1,0:T(8,128)(2,1)} %get-tuple-element.32.eo_ref, bf16[832,512]{1,0:T(8,128)(2,1)} %get-tuple-element.33.place_ref, ...), custom_call_target="tpu_custom_call" | custom-call | tf_op jit(solution)/shard_map/back/pallas_call | solution.py:812
  292.7 1.2 slice.75
  293.9 1.3 copy.39
  297.2 0.7 pad_maximum_fusion
  298.2 0.8 copy.50
  299.0 1.5 reshape.76
  300.6 1.6 copy.40
  302.2 1.0 copy.54
  (42 shorter events, 6.6 us)
Async XLA Ops:
  0.6 4.8 %copy-start.3 = (bf16[2,197,768]{2,0,1:T(2,128)(2,1)S(1)}, bf16[2,197,768]{2,0,1:T(2,128)(2,1)}, u32[]{:S(2)}) copy-start(bf16[2,197,768]{2,0,1:T(2,128)(2,1)} %param.11) | copy-start | bytes 1815556
  5.5 1.2 copy-start.4
  6.7 1.2 copy-start.5
  58.5 5.8 %slice-start = ((bf16[32,48,1664]{2,1,0:T(8,128)(2,1)}), bf16[32,48,128]{2,1,0:T(8,128)(2,1)S(1)}, s32[]{:S(2)}) async-start(bf16[32,48,1664]{2,1,0:T(8,128)(2,1)} %layer_gather.1), calls=%async_computation | async-start | bytes 786432 | tf_op jit(solution)/shard_map/slice | solution.py:877
  292.7 2.5 copy-start.7
  292.7 3.8 %copy-start.6 = (f32[4,24,768]{2,1,0:T(8,128)S(1)}, f32[4,24,768]{2,1,0:T(8,128)}, u32[]{:S(2)}) copy-start(f32[4,24,768]{2,1,0:T(8,128)} %get-tuple-element.42) | copy-start | bytes 884740
  293.9 4.0 %copy-start.2 = (f32[3,96,1024]{2,1,0:T(8,128)S(1)}, f32[3,96,1024]{2,1,0:T(8,128)}, u32[]{:S(2)}) copy-start(f32[3,96,1024]{2,1,0:T(8,128)} %get-tuple-element.43) | copy-start | bytes 3538948
  299.0 1.5 copy-start
  300.5 1.7 copy-start.1
